TPU v7x, 256 devices: a whole 4x4x8 slice. The times are simulated.
256 devices in a mesh: lon: 8 (over x, y_lo), lat: 32 (over y_hi, z, core).
Axes of the slice: x: 4, y: 4 (y_hi: 2, y_lo: 2; y = y_hi * 2 + y_lo), z: 8, core: 2. Of those that a mesh axis runs over, the one named last changes fastest.
Arguments:
- queries: bfloat16 [2, 64, 256, 2048], P(None, 'lat', 'lon'), may hold values from -4.5 to 4.5
- key_states: bfloat16 [2, 64, 256, 2048], P(None, 'lat', 'lon'), may hold values from -4.5 to 4.5
- value_states: bfloat16 [2, 64, 256, 2048], P(None, 'lat', 'lon'), may hold values from -6 to 6
- out_grad: bfloat16 [2, 64, 256, 2048], P(None, 'lat', 'lon'), may hold values from -6 to 6
- block_lists: int32 [32, 3], replicated, may hold values from -1 to 31, as said below
- row_widths: int32 [64], replicated, may hold values from 1 to 8, as said below
Outputs:
- attended: bfloat16 [2, 64, 256, 2048], P(None, 'lat', 'lon')
- query_grad: bfloat16 [2, 64, 256, 2048], P(None, 'lat', 'lon')
- key_grad: bfloat16 [2, 64, 256, 2048], P(None, 'lat', 'lon')
- value_grad: bfloat16 [2, 64, 256, 2048], P(None, 'lat', 'lon')
Inputs may be any that keep to these rules, and one draw needn't show every extreme that they name: `block_lists`: row t lists tile t itself and possibly t - 1 and t + 1 where they exist, each at most once, in any order; unused slots hold -1. The two tiles nearest each end list every existing neighbour. `row_widths`: the first and last 8 rows have half-width 8.
All inputs are finite; a program needn't handle non-finite values.
Results may differ from a plain program's by a relative error of at most 0.0067.
Values may be sent and summed in bfloat16 or wider, within the bound.
A program may use at most 64 MiB of HBM per device.

v0:
```python
import functools
import math

import jax
import jax.numpy as jnp
from jax import lax
from jax.experimental import pallas as pl
from jax.experimental.pallas import tpu as pltpu
from jax.sharding import PartitionSpec as P

MESH = pl.DeviceIdType.MESH
HALO = 8
HDIM = 128
GROUPS = 8
AHEAD = 5
BEHIND = 5
DETOURS = 2
HIDDEN = -1e30
FLOOR = -1e29


def nt(a, b):
    return lax.dot_general(a, b, (((1,), (1,)), ((), ())), preferred_element_type=jnp.float32)


def nn(a, b):
    return jnp.dot(a, b, preferred_element_type=jnp.float32)


def window(x, old, new, size, rest):
    lane = lax.broadcasted_iota(jnp.int32, x.shape, 1)
    shifted = x if old == new else pltpu.roll(x, (new - old) % HDIM, 1)
    return jnp.where((lane >= new) & (lane < new + size), shifted, rest)


def kernel(
    lon_count,
    lat_count,
    lists_hbm,
    widths_hbm,
    q_hbm,
    k_hbm,
    v_hbm,
    g_hbm,
    outs,
    near,
    edge_in,
    far,
    edge_out,
    bias,
    exps,
    dps,
    stats,
    stats_out,
    stats_in,
    factors,
    columns,
    mixed,
    near_acc,
    part_out,
    part_in,
    far_acc,
    term_out,
    term_in,
    relay,
    detour,
    lists_ref,
    widths_ref,
    small_sem,
    own_sem,
    kv_send,
    kv_recv,
    edge_send,
    edge_recv,
    stat_send,
    stat_recv,
    part_send,
    part_recv,
    term_send,
    term_recv,
    pass_send,
    pass_recv,
    relay_send,
    detour_send,
    detour_recv,
    ready,
):
    lon = lax.axis_index("lon")
    lat = lax.axis_index("lat")
    left = lax.rem(lon + lon_count - 1, lon_count)
    right = lax.rem(lon + 1, lon_count)
    has_above = lat > 0
    has_below = lat < lat_count - 1
    middle = lat_count // 2
    beside = lon + 1 - 2 * lax.rem(lon, 2)
    is_middle = (lat == middle - 1) | (lat == middle)
    routes = ((middle, 0, middle - 1), (middle - 1, lat_count - 1, middle))
    planes = middle // 2
    plane = lax.rem(lat // 2, planes)
    is_hot = (plane == 0) | (plane == planes - 1)
    is_detour = (plane == 1) | (plane == planes - 2)
    inward = jnp.where(plane < planes // 2, 2, -2)
    images, tokens, channels = q_hbm.shape
    heads = channels // HDIM
    group_heads = heads // GROUPS
    group_items = images * group_heads
    group_lanes = group_heads * HDIM
    scale = HDIM ** -0.5
    half = images // 2
    whole, direct, passing = slice(0, images), slice(0, half), slice(half, images)

    sides = ({"lon": left}, {"lon": right})
    tiles = ({"lat": lat - 1}, {"lat": lat + 1})
    exists = (has_above, has_below)

    barrier = pltpu.get_barrier_semaphore()
    for side in sides:
        pl.semaphore_signal(barrier, inc=1, device_id=side, device_id_type=MESH)
    below_middle = lat == middle
    teller = lat == middle - 2
    greets = (has_above, has_below & (lat != middle - 1))
    for there, tile in zip(greets, tiles):
        @pl.when(there)
        def _():
            pl.semaphore_signal(barrier, inc=1, device_id=tile, device_id_type=MESH)
    for here, place in ((below_middle, {"lat": middle - 2}), (lat == 0, {"lat": middle - 2, "lon": beside})):
        @pl.when(here)
        def _():
            pl.semaphore_signal(barrier, inc=1, device_id=place, device_id_type=MESH)
    for route in routes:
        @pl.when(lat == route[1])
        def _():
            pl.semaphore_signal(barrier, inc=1, device_id={"lat": route[0], "lon": beside}, device_id_type=MESH)
    @pl.when(is_detour)
    def _():
        for side in (left, right):
            pl.semaphore_signal(
                barrier, inc=1, device_id={"lat": lat - inward, "lon": side}, device_id_type=MESH
            )

    def lanes(group):
        start = group * group_lanes
        return pl.ds(start if isinstance(group, int) else pl.multiple_of(start, HDIM), group_lanes)

    def own_copies(group):
        targets = (far.at[group, 1, 0], far.at[group, 1, 1], near.at[group, 0], near.at[group, 1])
        return [
            pltpu.make_async_copy(source.at[:, :, lanes(group)], target, own_sem.at[group, which])
            for which, (source, target) in enumerate(zip((k_hbm, v_hbm, q_hbm, g_hbm), targets))
        ]

    def fetch(group, carry):
        for copy in own_copies(group):
            copy.start()
        return carry

    fetch(0, 0)
    small_copies = [
        pltpu.make_async_copy(lists_hbm, lists_ref, small_sem.at[0]),
        pltpu.make_async_copy(widths_hbm, widths_ref, small_sem.at[1]),
    ]
    for copy in small_copies:
        copy.start()

    lax.fori_loop(1, GROUPS, fetch, 0)

    pl.semaphore_wait(
        barrier,
        2 + jnp.where(has_above & (lat != middle), 1, 0) + jnp.where(has_below, 1, 0) + jnp.where(is_middle, 1, 0)
        + jnp.where(is_hot, 2, 0)
        + jnp.where(teller, 2, 0),
    )

    @pl.when(teller)
    def _():
        pl.semaphore_signal(ready, inc=1, device_id={"lat": middle}, device_id_type=MESH)
        pl.semaphore_signal(ready, inc=1, device_id={"lat": 0, "lon": beside}, device_id_type=MESH)


    def remote(source, target, send, recv, device):
        return pltpu.make_async_remote_copy(
            src_ref=source, dst_ref=target, send_sem=send, recv_sem=recv, device_id=device, device_id_type=MESH
        )

    def kv_copy(group, way, some):
        return remote(
            far.at[group, 1, :, some],
            far.at[group, 2 - 2 * way, :, some],
            kv_send.at[way],
            kv_recv.at[group, 1 - way],
            tiles[way],
        )

    def edge_copy(group, way):
        return remote(
            edge_out.at[group, way],
            edge_in.at[group, 1 - way],
            edge_send.at[way],
            edge_recv.at[group, 1 - way],
            sides[way],
        )

    def stat_copy(group, way):
        return remote(
            stats_out.at[way, group, 0:group_items],
            stats_in.at[1 - way, group, 0:group_items],
            stat_send.at[way],
            stat_recv.at[group, 1 - way],
            sides[way],
        )

    def part_copy(group, way):
        return remote(
            part_out.at[group, way],
            part_in.at[group, 1 - way],
            part_send.at[way],
            part_recv.at[group, 1 - way],
            sides[way],
        )

    def term_copy(group, way, some):
        return remote(
            term_out.at[group, way, :, some],
            term_in.at[group, 1 - way, :, some],
            term_send.at[group, way],
            term_recv.at[group, 1 - way],
            tiles[way],
        )

    def pass_copy(group, way, kind):
        return remote(
            far.at[group, 1, :, passing] if kind == 0 else term_out.at[group, way, :, passing],
            relay.at[kind, group],
            pass_send.at[group, kind],
            pass_recv.at[group, kind],
            {"lat": routes[way][1], "lon": beside},
        )

    def relay_copy(group, way, kind):
        return remote(
            relay.at[kind, group],
            far.at[group, 2 - 2 * way, :, passing]
            if kind == 0
            else term_in.at[group, 1 - way, :, passing],
            relay_send.at[group, kind],
            (kv_recv if kind == 0 else term_recv).at[group, 1 - way],
            {"lat": routes[way][2], "lon": beside},
        )

    def detour_in(group, way, kind):
        which = group // 2 - 1
        return remote(
            (edge_out, part_out)[kind].at[group, way],
            detour.at[kind, which, 1 - way],
            (edge_send, part_send)[kind].at[way],
            detour_recv.at[kind, which, 1 - way],
            {"lat": lat + inward, "lon": (left, right)[way]},
        )

    def detour_out(group, origin, kind):
        which = group // 2 - 1
        return remote(
            detour.at[kind, which, origin],
            (edge_in, part_in)[kind].at[group, origin],
            detour_send.at[kind, which, origin],
            (edge_recv, part_recv)[kind].at[group, origin],
            {"lat": lat - inward},
        )

    def to_sides(group, kind):
        aside = is_hot & ((group == 2) | (group == 4))
        for way in range(2):
            @pl.when(jnp.logical_not(aside))
            def _():
                (edge_copy, part_copy)[kind](group, way).start()

            @pl.when(aside)
            def _():
                detour_in(group, way, kind).start()

    def pass_aside(group, kind):
        for origin in range(2):
            detour_in(group, 1 - origin, kind).wait_recv()
            detour_out(group, origin, kind).start()

    def relayed(group, kind):
        return True if kind == 0 else group < GROUPS - 2

    def to_tiles(group, kind, act):
        copy = (kv_copy, term_copy)[kind]
        for way in range(2):
            crossing = (lat == routes[way][0]) & relayed(group, kind)

            @pl.when(exists[way] & jnp.logical_not(crossing))
            def _():
                act(copy(group, way, whole))

            @pl.when(crossing)
            def _():
                if kind == 1 or way == 1:
                    act(copy(group, way, direct))
                act(pass_copy(group, way, kind))

    def from_tiles(group, kind):
        copy = (kv_copy, term_copy)[kind]
        for origin in range(2):
            @pl.when(exists[origin])
            def _():
                copy(group, 1 - origin, whole).wait_recv()

    def forward(group, kind):
        for way in range(2):
            @pl.when((lat == routes[way][1]) & relayed(group, kind))
            def _():
                pass_copy(group, way, kind).wait_recv()
                relay_copy(group, way, kind).start()

    def start(copy):
        copy.start()

    def wait_send(copy):
        copy.wait_send()

    def send_edges(group):
        for which in range(2):
            for image in range(images):
                def half(start, low):
                    block = near[group, which, image, start : start + 16].astype(jnp.float32)
                    return block[low : low + HALO]

                edge_out[group, 0, which, image] = jnp.concatenate(
                    [half(0, 0), half(32, 0)], axis=0
                ).astype(jnp.bfloat16)
                edge_out[group, 1, which, image] = jnp.concatenate(
                    [half(16, HALO), half(48, HALO)], axis=0
                ).astype(jnp.bfloat16)
        to_sides(group, 0)

    def send_group(group, carry):
        copies = own_copies(group)
        copies[0].wait()
        copies[1].wait()
        to_tiles(group, 0, start)
        copies[2].wait()
        copies[3].wait()

        @pl.when(group < AHEAD)
        def _():
            send_edges(group)

        return carry

    lax.fori_loop(0, GROUPS, send_group, 0)

    def send_above(group, carry):
        kv_copy(group, 0, direct).start()
        return carry

    for way in range(2):
        @pl.when(jnp.logical_not(exists[way]))
        def _():
            far[:, 2 * way] = jnp.zeros((GROUPS, 2, images, tokens, group_lanes), jnp.bfloat16)
            term_in[:, way] = jnp.zeros((GROUPS, 2, images, tokens, group_lanes), jnp.bfloat16)

    def listed(target):
        found = (
            (lists_ref[0, lat] == target)
            | (lists_ref[1, lat] == target)
            | (lists_ref[2, lat] == target)
        ) & (target >= 0)
        return jnp.where(found, 1, 0)

    def mask(shape, key_axis):
        key = lax.broadcasted_iota(jnp.int32, shape, key_axis)
        query = lax.broadcasted_iota(jnp.int32, shape, 1 - key_axis)
        key_tile = key >> 6
        key_col = key & 31
        edge = query - tokens
        is_own = query < tokens
        from_left = edge < 2 * HALO
        query_col = jnp.where(
            is_own, query & 31, jnp.where(from_left, (edge & 7) - HALO, 32 + (edge & 7))
        )
        query_row = jnp.where(is_own, query >> 5, (edge >> 3) & 1)
        width = jnp.where(query_row == 0, widths_ref[2 * lat], widths_ref[2 * lat + 1])
        active = jnp.where(
            key_tile == 0, listed(lat - 1), jnp.where(key_tile == 1, listed(lat), listed(lat + 1))
        )
        visible = (jnp.abs(query_col - key_col) <= width) & (active == 1) & (edge < 4 * HALO)
        return jnp.where(visible, 0.0, HIDDEN)

    for copy in small_copies:
        copy.wait()
    bias[...] = mask(bias.shape, 0)

    places = [(image, head) for image in range(images) for head in range(group_heads)]

    def from_near(group, which, image, head):
        at = pl.ds(head * HDIM, HDIM)
        edges = [edge_in[group, origin, which, image, :, at] for origin in range(2)]
        rest = jnp.zeros((2 * tokens - seen, HDIM), jnp.bfloat16)
        return jnp.concatenate([near[group, which, image, :, at]] + edges + [rest], axis=0)

    def from_far(group, which, image, head):
        at = pl.ds(head * HDIM, HDIM)
        return jnp.concatenate([far[group, slot, which, image, :, at] for slot in range(3)], axis=0)

    to_log2 = scale * math.log2(math.e)
    seen = tokens + 4 * HALO

    def scores(group):
        tops, sums, balances = [], [], []
        for item, (image, head) in enumerate(places):
            values = from_far(group, 1, image, head)
            raw = nt(from_far(group, 0, image, head), from_near(group, 0, image, head))
            raw = raw * to_log2 + bias[...]
            dp = nt(values, from_near(group, 1, image, head))
            top = jnp.maximum(jnp.max(raw, axis=0, keepdims=True), FLOOR)
            e = jnp.exp2(raw - top)
            slot = group * group_items + item
            exps[slot] = e
            dps[slot] = dp
            mixed[slot] = nn(jnp.transpose(e.astype(jnp.bfloat16))[0:seen], values)
            tops.append(top)
            sums.append(jnp.sum(e, axis=0, keepdims=True))
            balances.append(jnp.sum(e * dp, axis=0, keepdims=True))
        for kind, found in enumerate((tops, sums, balances)):
            rows = found + [jnp.zeros_like(found[0])] * (8 - len(found))
            stats[group, kind] = jnp.concatenate(rows, axis=0)
        for way, moves in enumerate((((0, 0, 8), (32, 8, 8), (64, 16, 16)), ((24, 0, 8), (56, 8, 8), (80, 16, 16)))):
            packed = jnp.zeros((8, HDIM), jnp.float32)
            for kind in range(3):
                for old, new, size in moves:
                    packed = window(stats[group, kind], old, 32 * kind + new, size, packed)
            stats_out[way, group] = packed
        for way in range(2):
            stat_copy(group, way).start()

    def wait_stats(group):
        for way in range(2):
            stat_copy(group, way).wait_recv()

    def combine(group):
        others = []
        for kind in range(3):
            other = jnp.full((8, HDIM), FLOOR if kind == 0 else 0.0, jnp.float32)
            for origin, moves in enumerate((((0, 64, 16), (16, 0, 8), (24, 32, 8)), ((0, 80, 16), (16, 24, 8), (24, 56, 8)))):
                for old, new, size in moves:
                    other = window(stats_in[origin, group], 32 * kind + old, new, size, other)
            others.append(other)
        top, total, balance = (stats[group, kind] for kind in range(3))
        top2, total2, balance2 = others
        high = jnp.maximum(top, top2)
        part = jnp.exp2(top - high)
        part2 = jnp.exp2(top2 - high)
        inverse = 1.0 / jnp.maximum(part * total + part2 * total2, 0.5)
        factor = part * inverse
        factors[group, 0] = factor
        factors[group, 1] = (part * balance + part2 * balance2) * inverse
        columns[group] = jnp.transpose(factor)

    def gradients(group):
        for item, (image, head) in enumerate(places):
            at = pl.ds(head * HDIM, HDIM)
            slot = group * group_items + item
            keys = from_far(group, 0, image, head)
            queries, grads = (from_near(group, which, image, head) for which in range(2))
            w = exps[slot] * factors[group, 0, item : item + 1, :]
            ds = w * (dps[slot] - factors[group, 1, item : item + 1, :])
            w = w.astype(jnp.bfloat16)
            ds = ds.astype(jnp.bfloat16)
            dk = nn(ds, queries) * scale
            dv = nn(w, grads)
            att = mixed[slot] * columns[group, 0:seen, item : item + 1]
            dq = nn(jnp.transpose(ds)[0:seen], keys) * scale
            for which, x in enumerate((dk, dv)):
                far_acc[group, which, image, :, at] = x[tokens : 2 * tokens]
                term_out[group, 0, which, image, :, at] = x[0:tokens].astype(jnp.bfloat16)
                term_out[group, 1, which, image, :, at] = x[2 * tokens :].astype(jnp.bfloat16)
            for which, x in enumerate((att, dq)):
                near_acc[group, which, image, :, at] = x[0:tokens]
                for way in range(2):
                    low = tokens + 2 * HALO * way
                    part_out[group, way, which, image, :, at] = x[low : low + 2 * HALO].astype(jnp.bfloat16)
        to_tiles(group, 1, start)
        to_sides(group, 1)

    def finish(group):
        for way in range(2):
            part_copy(group, way).wait_recv()
        from_tiles(group, 1)
        at = lanes(group)
        for image in range(images):
            for which in range(2):
                acc = near_acc[group, which, image]
                add_l = part_in[group, 0, which, image].astype(jnp.float32)
                add_r = part_in[group, 1, which, image].astype(jnp.float32)
                rows = []
                for r in range(2):
                    here = acc[32 * r : 32 * r + 32]
                    rows.append(here[0:8] + add_l[8 * r : 8 * r + 8])
                    rows.append(here[8:24])
                    rows.append(here[24:32] + add_r[8 * r : 8 * r + 8])
                outs[which, image, :, at] = jnp.concatenate(rows, axis=0).astype(jnp.bfloat16)
            for which in range(2):
                total = far_acc[group, which, image]
                for way in range(2):
                    total = total + term_in[group, way, which, image].astype(jnp.float32)
                outs[2 + which, image, :, at] = total.astype(jnp.bfloat16)

    def step(index, carry):
        @pl.when(index < GROUPS // 2)
        def _():
            forward(2 * index, 0)
            forward(2 * index + 1, 0)

        for group in (2, 4):
            @pl.when(is_detour & (index == group + 1))
            def _():
                pass_aside(group, 0)

        @pl.when(index < GROUPS)
        def _():
            from_tiles(index, 0)
            for origin in range(2):
                edge_copy(index, 1 - origin).wait_recv()

            scores(index)

            @pl.when(index + AHEAD < GROUPS)
            def _():
                send_edges(index + AHEAD)

        @pl.when((index >= BEHIND + 2) & (index < GROUPS + BEHIND))
        def _():
            forward(index - BEHIND - 2, 1)

        @pl.when(index >= BEHIND)
        def _():
            wait_stats(index - BEHIND)
            combine(index - BEHIND)
            gradients(index - BEHIND)

        return carry

    @pl.when(below_middle | (lat == 0))
    def _():
        pl.semaphore_wait(ready, 1)

    @pl.when(below_middle)
    def _():
        lax.fori_loop(0, GROUPS, send_above, 0)

    lax.fori_loop(0, GROUPS + BEHIND, step, 0)

    @pl.when(is_detour)
    def _():
        for group in (2, 4):
            pass_aside(group, 1)

    def last(group, carry):
        finish(group)
        return carry

    lax.fori_loop(0, GROUPS, last, 0)

    def drain(group, carry):
        to_tiles(group, 1, wait_send)
        for way in range(2):
            @pl.when(lat == routes[way][0])
            def _():
                pass_copy(group, way, 0).wait_send()

        for kind in range(2):
            for way in range(2):
                @pl.when((lat == routes[way][1]) & relayed(group, kind))
                def _():
                    relay_copy(group, way, kind).wait_send()
        return carry

    lax.fori_loop(0, GROUPS, drain, 0)
    @pl.when(is_detour)
    def _():
        for kind in range(2):
            for group in (2, 4):
                for origin in range(2):
                    detour_out(group, origin, kind).wait_send()

    for way in range(2):
        for source, sem in (
            (edge_out.at[:, way], edge_send.at[way]),
            (part_out.at[:, way], part_send.at[way]),
            (stats_out.at[way, :, 0:group_items], stat_send.at[way]),
        ):
            remote(source, source, sem, sem, sides[way]).wait_send()
        crossing = lat == routes[way][0]
        for some, here in ((whole, jnp.logical_not(crossing)), (direct, crossing)):
            @pl.when(exists[way] & here)
            def _():
                sent = far.at[:, 1, :, some]
                remote(sent, sent, kv_send.at[way], kv_send.at[way], tiles[way]).wait_send()


def split_kernel(stacked, *refs):
    outs, sem = refs[:4], refs[4]
    copies = [pltpu.make_async_copy(stacked.at[i], outs[i], sem.at[i]) for i in range(4)]
    for copy in copies:
        copy.start()
    for copy in copies:
        copy.wait()


def solution(mesh):
    lon_count = mesh.shape["lon"]
    lat_count = mesh.shape["lat"]

    def on_device(queries, key_states, value_states, out_grad, block_lists, row_widths):
        images, rows, columns, channels = queries.shape
        tokens = rows * columns
        flat = (images, tokens, channels)
        items = images * channels // HDIM
        lanes = channels // GROUPS
        bf16, f32 = jnp.bfloat16, jnp.float32
        hbm_spec = pl.BlockSpec(memory_space=pltpu.HBM)
        vmem_spec = pl.BlockSpec(memory_space=pltpu.VMEM)
        dma = pltpu.SemaphoreType.DMA
        stacked = pl.pallas_call(
            functools.partial(kernel, lon_count, lat_count),
            out_shape=pltpu.VMEM((4,) + flat, bf16),
            in_specs=[hbm_spec] * 6,
            out_specs=vmem_spec,
            scratch_shapes=[
                pltpu.VMEM((GROUPS, 2, images, tokens, lanes), bf16),
                pltpu.VMEM((GROUPS, 2, 2, images, 2 * HALO, lanes), bf16),
                pltpu.VMEM((GROUPS, 3, 2, images, tokens, lanes), bf16),
                pltpu.VMEM((GROUPS, 2, 2, images, 2 * HALO, lanes), bf16),
                pltpu.VMEM((3 * tokens, 2 * tokens), f32),
                pltpu.VMEM((items, 3 * tokens, 2 * tokens), f32),
                pltpu.VMEM((items, 3 * tokens, 2 * tokens), f32),
                pltpu.VMEM((GROUPS, 3, 8, 2 * tokens), f32),
                pltpu.VMEM((2, GROUPS, 8, 2 * tokens), f32),
                pltpu.VMEM((2, GROUPS, 8, 2 * tokens), f32),
                pltpu.VMEM((GROUPS, 2, 8, 2 * tokens), f32),
                pltpu.VMEM((GROUPS, 2 * tokens, 8), f32),
                pltpu.VMEM((items, tokens + 4 * HALO, HDIM), f32),
                pltpu.VMEM((GROUPS, 2, images, tokens, lanes), f32),
                pltpu.VMEM((GROUPS, 2, 2, images, 2 * HALO, lanes), bf16),
                pltpu.VMEM((GROUPS, 2, 2, images, 2 * HALO, lanes), bf16),
                pltpu.VMEM((GROUPS, 2, images, tokens, lanes), f32),
                pltpu.VMEM((GROUPS, 2, 2, images, tokens, lanes), bf16),
                pltpu.VMEM((GROUPS, 2, 2, images, tokens, lanes), bf16),
                pltpu.VMEM((2, GROUPS, 2, images - images // 2, tokens, lanes), bf16),
                pltpu.VMEM((2, DETOURS, 2, 2, images, 2 * HALO, lanes), bf16),
                pltpu.SMEM(block_lists.shape[::-1], jnp.int32),
                pltpu.SMEM(row_widths.shape, jnp.int32),
                dma((2,)),
                dma((GROUPS, 4)),
                dma((2,)),
                dma((GROUPS, 2)),
                dma((2,)),
                dma((GROUPS, 2)),
                dma((2,)),
                dma((GROUPS, 2)),
                dma((2,)),
                dma((GROUPS, 2)),
                dma((GROUPS, 2)),
                dma((GROUPS, 2)),
                dma((GROUPS, 2)),
                dma((GROUPS, 2)),
                dma((GROUPS, 2)),
                dma((2, DETOURS, 2)),
                dma((2, DETOURS, 2)),
                pltpu.SemaphoreType.REGULAR,
            ],
            compiler_params=pltpu.CompilerParams(
                collective_id=0, has_side_effects=True, vmem_limit_bytes=60 * 1024 * 1024
            ),
            cost_estimate=pl.CostEstimate(
                flops=12 * items * 192 * 128 * 128,
                bytes_accessed=8 * images * tokens * channels * 2,
                transcendentals=items * 192 * 128,
            ),
        )(
            block_lists.T,
            row_widths,
            queries.reshape(flat),
            key_states.reshape(flat),
            value_states.reshape(flat),
            out_grad.reshape(flat),
        )
        results = pl.pallas_call(
            split_kernel,
            out_shape=[jax.ShapeDtypeStruct(flat, bf16)] * 4,
            in_specs=[pl.BlockSpec(memory_space=pl.ANY)],
            out_specs=[hbm_spec] * 4,
            scratch_shapes=[dma((4,))],
            compiler_params=pltpu.CompilerParams(vmem_limit_bytes=8 * 1024 * 1024),
        )(stacked)
        return tuple(x.reshape(queries.shape) for x in results)

    split = P(None, "lat", "lon", None)
    return jax.shard_map(
        on_device,
        mesh=mesh,
        in_specs=(split, split, split, split, P(), P()),
        out_specs=(split, split, split, split),
        check_vma=False,
    )
```

profile of v0, /device:TPU:2, one launch (start us, length us, event | category | flops | bytes accessed | tf_op | source)
XLA Modules:
  0.0 46.9 jit_solution(11752744660008855156)
XLA Ops:
  0.6 45.0 %shard_map.93.stacked = bf16[4,2,64,2048]{3,2,1,0:T(8,128)(2,1)S(1)} custom-call(s32[3,32]{1,0:T(4,128)} %bitcast.17, s32[64]{0:T(128)} %widths_hbm.1, bf16[2,64,2048]{2,1,0:T(8,128)(2,1)} %bitcast.9, bf16[2,64,2048]{2,1,0:T(8,128)(2,1)} %bitcast.10, bf16[2,64,2048]{2,1,0:T(8,128)(2,1)} %bitcast.11, bf16[2,64,2048]{2,1,0:T(8,128)(2,1)} %bitcast.12), custom_call_target="tpu_custom_call" | custom-call | flops 1207959552 | bytes 4194304 | tf_op jit(solution)/shard_map/pallas_call | solution.py:627
  45.6 1.3 %shard_map.94 = (bf16[2,64,2048]{2,1,0:T(8,128)(2,1)}, bf16[2,64,2048]{2,1,0:T(8,128)(2,1)}, bf16[2,64,2048]{2,1,0:T(8,128)(2,1)}, bf16[2,64,2048]{2,1,0:T(8,128)(2,1)}) custom-call(bf16[4,2,64,2048]{3,2,1,0:T(8,128)(2,1)S(1)} %shard_map.93.stacked), custom_call_target="tpu_custom_call" | custom-call | tf_op jit(solution)/shard_map/pallas_call | solution.py:691
where the time goes:
time: 47.1 us; the launch traced here: 46.9 us
  Pallas kernels  46.3 us (98%)
  between operations  0.64 us (1%)
    pallas_call x1, Pallas kernels, on_device(): pl.pallas_call(functools.partial(kernel, lon_count, lat_count), out_shape...  45 us
    pallas_call x1, Pallas kernels, on_device(): pl.pallas_call(split_kernel, out_shape=[jax.ShapeDtypeStruct(flat, bf16)]...  1.35 us

commit v1 on v0

--- a/solution.py
+++ b/solution.py
@@ -77,6 +77,7 @@
     part_send,
     part_recv,
     term_send,
+    half_send,
     term_recv,
     pass_send,
     pass_recv,
@@ -222,7 +223,7 @@
         return remote(
             term_out.at[group, way, :, some],
             term_in.at[group, 1 - way, :, some],
-            term_send.at[group, way],
+            (term_send if some is whole else half_send).at[way],
             term_recv.at[group, 1 - way],
             tiles[way],
         )
@@ -231,7 +232,7 @@
         return remote(
             far.at[group, 1, :, passing] if kind == 0 else term_out.at[group, way, :, passing],
             relay.at[kind, group],
-            pass_send.at[group, kind],
+            pass_send.at[kind],
             pass_recv.at[group, kind],
             {"lat": routes[way][1], "lon": beside},
         )
@@ -242,7 +243,7 @@
             far.at[group, 2 - 2 * way, :, passing]
             if kind == 0
             else term_in.at[group, 1 - way, :, passing],
-            relay_send.at[group, kind],
+            relay_send.at[kind],
             (kv_recv if kind == 0 else term_recv).at[group, 1 - way],
             {"lat": routes[way][2], "lon": beside},
         )
@@ -317,9 +318,6 @@
 
     def start(copy):
         copy.start()
-
-    def wait_send(copy):
-        copy.wait_send()
 
     def send_edges(group):
         for which in range(2):
@@ -564,21 +562,9 @@
 
     lax.fori_loop(0, GROUPS, last, 0)
 
-    def drain(group, carry):
-        to_tiles(group, 1, wait_send)
-        for way in range(2):
-            @pl.when(lat == routes[way][0])
-            def _():
-                pass_copy(group, way, 0).wait_send()
-
-        for kind in range(2):
-            for way in range(2):
-                @pl.when((lat == routes[way][1]) & relayed(group, kind))
-                def _():
-                    relay_copy(group, way, kind).wait_send()
-        return carry
-
-    lax.fori_loop(0, GROUPS, drain, 0)
+    def sent(source, sem):
+        remote(source, source, sem, sem, sides[0]).wait_send()
+
     @pl.when(is_detour)
     def _():
         for kind in range(2):
@@ -592,13 +578,26 @@
             (part_out.at[:, way], part_send.at[way]),
             (stats_out.at[way, :, 0:group_items], stat_send.at[way]),
         ):
-            remote(source, source, sem, sem, sides[way]).wait_send()
+            sent(source, sem)
         crossing = lat == routes[way][0]
-        for some, here in ((whole, jnp.logical_not(crossing)), (direct, crossing)):
-            @pl.when(exists[way] & here)
-            def _():
-                sent = far.at[:, 1, :, some]
-                remote(sent, sent, kv_send.at[way], kv_send.at[way], tiles[way]).wait_send()
+
+        @pl.when(exists[way] & jnp.logical_not(crossing))
+        def _():
+            sent(far.at[:, 1], kv_send.at[way])
+            sent(term_out.at[:, way], term_send.at[way])
+
+        @pl.when(crossing)
+        def _():
+            sent(far.at[:, 1, :, direct], kv_send.at[way])
+            sent(far.at[:, 1, :, passing], pass_send.at[0])
+            sent(term_out.at[0 : GROUPS - 2, way, :, direct], half_send.at[way])
+            sent(term_out.at[0 : GROUPS - 2, way, :, passing], pass_send.at[1])
+            sent(term_out.at[GROUPS - 2 :, way], term_send.at[way])
+
+        @pl.when(lat == routes[way][1])
+        def _():
+            sent(relay.at[0], relay_send.at[0])
+            sent(relay.at[1, 0 : GROUPS - 2], relay_send.at[1])
 
 
 def split_kernel(stacked, *refs):
@@ -663,11 +662,12 @@
                 dma((GROUPS, 2)),
                 dma((2,)),
                 dma((GROUPS, 2)),
+                dma((2,)),
+                dma((2,)),
                 dma((GROUPS, 2)),
+                dma((2,)),
                 dma((GROUPS, 2)),
-                dma((GROUPS, 2)),
-                dma((GROUPS, 2)),
-                dma((GROUPS, 2)),
+                dma((2,)),
                 dma((2, DETOURS, 2)),
                 dma((2, DETOURS, 2)),
                 pltpu.SemaphoreType.REGULAR,

time: 47.1 us -> 46.5 us (0.987)
  Pallas kernels: 46.3 us -> 45.7 us
    pallas_call x1, Pallas kernels: 45 us -> 44.3 us  [on_device(): pl.pallas_call(functools.partial(kernel, lon_count, lat_count), out_shape...]
where the time goes in v1:
time: 46.5 us; the launch traced here: 46.3 us
  Pallas kernels  45.7 us (98%)
  between operations  0.64 us (1%)
    pallas_call x1, Pallas kernels, on_device(): pl.pallas_call(functools.partial(kernel, lon_count, lat_count), out_shape...  44.3 us
    pallas_call x1, Pallas kernels, on_device(): pl.pallas_call(split_kernel, out_shape=[jax.ShapeDtypeStruct(flat, bf16)]...  1.35 us

profile of v1, /device:TPU:2, one launch (start us, length us, event | category | flops | bytes accessed | tf_op | source)
XLA Modules:
  0.0 46.3 jit_solution(11387417855507229863)
XLA Ops:
  0.6 44.3 %shard_map.93.stacked = bf16[4,2,64,2048]{3,2,1,0:T(8,128)(2,1)S(1)} custom-call(s32[3,32]{1,0:T(4,128)} %bitcast.17, s32[64]{0:T(128)} %widths_hbm.1, bf16[2,64,2048]{2,1,0:T(8,128)(2,1)} %bitcast.9, bf16[2,64,2048]{2,1,0:T(8,128)(2,1)} %bitcast.10, bf16[2,64,2048]{2,1,0:T(8,128)(2,1)} %bitcast.11, bf16[2,64,2048]{2,1,0:T(8,128)(2,1)} %bitcast.12), custom_call_target="tpu_custom_call" | custom-call | flops 1207959552 | bytes 4194304 | tf_op jit(solution)/shard_map/pallas_call | solution.py:626
  45.0 1.3 %shard_map.94 = (bf16[2,64,2048]{2,1,0:T(8,128)(2,1)}, bf16[2,64,2048]{2,1,0:T(8,128)(2,1)}, bf16[2,64,2048]{2,1,0:T(8,128)(2,1)}, bf16[2,64,2048]{2,1,0:T(8,128)(2,1)}) custom-call(bf16[4,2,64,2048]{3,2,1,0:T(8,128)(2,1)S(1)} %shard_map.93.stacked), custom_call_target="tpu_custom_call" | custom-call | tf_op jit(solution)/shard_map/pallas_call | solution.py:691

commit v2 on v1

--- a/solution.py
+++ b/solution.py
@@ -284,13 +284,15 @@
             detour_in(group, 1 - origin, kind).wait_recv()
             detour_out(group, origin, kind).start()
 
-    def relayed(group, kind):
-        return True if kind == 0 else group < GROUPS - 2
+    relayed_terms = (GROUPS - 2, GROUPS - 1)
+
+    def relayed(group, kind, way):
+        return True if kind == 0 else group < relayed_terms[way]
 
     def to_tiles(group, kind, act):
         copy = (kv_copy, term_copy)[kind]
         for way in range(2):
-            crossing = (lat == routes[way][0]) & relayed(group, kind)
+            crossing = (lat == routes[way][0]) & relayed(group, kind, way)
 
             @pl.when(exists[way] & jnp.logical_not(crossing))
             def _():
@@ -311,7 +313,7 @@
 
     def forward(group, kind):
         for way in range(2):
-            @pl.when((lat == routes[way][1]) & relayed(group, kind))
+            @pl.when((lat == routes[way][1]) & relayed(group, kind, way))
             def _():
                 pass_copy(group, way, kind).wait_recv()
                 relay_copy(group, way, kind).start()
@@ -556,6 +558,8 @@
         for group in (2, 4):
             pass_aside(group, 1)
 
+    forward(GROUPS - 2, 1)
+
     def last(group, carry):
         finish(group)
         return carry
@@ -590,14 +594,15 @@
         def _():
             sent(far.at[:, 1, :, direct], kv_send.at[way])
             sent(far.at[:, 1, :, passing], pass_send.at[0])
-            sent(term_out.at[0 : GROUPS - 2, way, :, direct], half_send.at[way])
-            sent(term_out.at[0 : GROUPS - 2, way, :, passing], pass_send.at[1])
-            sent(term_out.at[GROUPS - 2 :, way], term_send.at[way])
+            count = relayed_terms[way]
+            sent(term_out.at[0:count, way, :, direct], half_send.at[way])
+            sent(term_out.at[0:count, way, :, passing], pass_send.at[1])
+            sent(term_out.at[count:, way], term_send.at[way])
 
         @pl.when(lat == routes[way][1])
         def _():
             sent(relay.at[0], relay_send.at[0])
-            sent(relay.at[1, 0 : GROUPS - 2], relay_send.at[1])
+            sent(relay.at[1, 0 : relayed_terms[way]], relay_send.at[1])
 
 
 def split_kernel(stacked, *refs):

time: 46.5 us -> 48 us (1.032)
  the two profiles are of different devices: /device:TPU:2 before, /device:TPU:16 now
where the time goes in v2:
time: 48 us; the launch traced here: 47.9 us
  Pallas kernels  47.2 us (98%)
  between operations  0.64 us (1%)
    pallas_call x1, Pallas kernels, on_device(): pl.pallas_call(functools.partial(kernel, lon_count, lat_count), out_shape...  45.9 us
    pallas_call x1, Pallas kernels, on_device(): pl.pallas_call(split_kernel, out_shape=[jax.ShapeDtypeStruct(flat, bf16)]...  1.35 us

profile of v2, /device:TPU:16, one launch (start us, length us, event | category | flops | bytes accessed | tf_op | source)
XLA Modules:
  0.0 47.9 jit_solution(5413724936411257996)
XLA Ops:
  0.6 45.9 %shard_map.93.stacked = bf16[4,2,64,2048]{3,2,1,0:T(8,128)(2,1)S(1)} custom-call(s32[3,32]{1,0:T(4,128)} %bitcast.17, s32[64]{0:T(128)} %widths_hbm.1, bf16[2,64,2048]{2,1,0:T(8,128)(2,1)} %bitcast.9, bf16[2,64,2048]{2,1,0:T(8,128)(2,1)} %bitcast.10, bf16[2,64,2048]{2,1,0:T(8,128)(2,1)} %bitcast.11, bf16[2,64,2048]{2,1,0:T(8,128)(2,1)} %bitcast.12), custom_call_target="tpu_custom_call" | custom-call | flops 1207959552 | bytes 4194304 | tf_op jit(solution)/shard_map/pallas_call | solution.py:631
  46.5 1.3 %shard_map.94 = (bf16[2,64,2048]{2,1,0:T(8,128)(2,1)}, bf16[2,64,2048]{2,1,0:T(8,128)(2,1)}, bf16[2,64,2048]{2,1,0:T(8,128)(2,1)}, bf16[2,64,2048]{2,1,0:T(8,128)(2,1)}) custom-call(bf16[4,2,64,2048]{3,2,1,0:T(8,128)(2,1)S(1)} %shard_map.93.stacked), custom_call_target="tpu_custom_call" | custom-call | tf_op jit(solution)/shard_map/pallas_call | solution.py:696

commit v3 on v1

--- a/solution.py
+++ b/solution.py
@@ -12,7 +12,7 @@
 HALO = 8
 HDIM = 128
 GROUPS = 8
-AHEAD = 5
+AHEAD = 6
 BEHIND = 5
 DETOURS = 2
 HIDDEN = -1e30

time: 46.5 us -> 46.2 us (level)
  no operation moved by 1% of the time
where the time goes in v3:
time: 46.2 us; the launch traced here: 46.1 us
  Pallas kernels  45.4 us (98%)
  between operations  0.64 us (1%)
    pallas_call x1, Pallas kernels, on_device(): pl.pallas_call(functools.partial(kernel, lon_count, lat_count), out_shape...  44.1 us
    pallas_call x1, Pallas kernels, on_device(): pl.pallas_call(split_kernel, out_shape=[jax.ShapeDtypeStruct(flat, bf16)]...  1.35 us

profile of v3, /device:TPU:2, one launch (start us, length us, event | category | flops | bytes accessed | tf_op | source)
XLA Modules:
  0.0 46.1 jit_solution(2602939131562782532)
XLA Ops:
  0.6 44.1 %shard_map.93.stacked = bf16[4,2,64,2048]{3,2,1,0:T(8,128)(2,1)S(1)} custom-call(s32[3,32]{1,0:T(4,128)} %bitcast.17, s32[64]{0:T(128)} %widths_hbm.1, bf16[2,64,2048]{2,1,0:T(8,128)(2,1)} %bitcast.9, bf16[2,64,2048]{2,1,0:T(8,128)(2,1)} %bitcast.10, bf16[2,64,2048]{2,1,0:T(8,128)(2,1)} %bitcast.11, bf16[2,64,2048]{2,1,0:T(8,128)(2,1)} %bitcast.12), custom_call_target="tpu_custom_call" | custom-call | flops 1207959552 | bytes 4194304 | tf_op jit(solution)/shard_map/pallas_call | solution.py:626
  44.7 1.3 %shard_map.94 = (bf16[2,64,2048]{2,1,0:T(8,128)(2,1)}, bf16[2,64,2048]{2,1,0:T(8,128)(2,1)}, bf16[2,64,2048]{2,1,0:T(8,128)(2,1)}, bf16[2,64,2048]{2,1,0:T(8,128)(2,1)}) custom-call(bf16[4,2,64,2048]{3,2,1,0:T(8,128)(2,1)S(1)} %shard_map.93.stacked), custom_call_target="tpu_custom_call" | custom-call | tf_op jit(solution)/shard_map/pallas_call | solution.py:691
